TPU v7x, 256 devices: a whole 4x4x8 slice. The times are simulated.
256 devices in a mesh: cfg: 2 (over core), blk: 16 (over z, x_lo), uly: 8 (over x_hi, y).
Axes of the slice: x: 4 (x_hi: 2, x_lo: 2; x = x_hi * 2 + x_lo), y: 4, z: 8, core: 2. Of those that a mesh axis runs over, the one named last changes fastest.
Arguments:
- queries: bfloat16 [2, 8192, 5120], P('cfg', ('blk', 'uly')), may hold values from -6 to 6
- keys: bfloat16 [2, 8192, 5120], P('cfg', ('blk', 'uly')), may hold values from -6 to 6
- values: bfloat16 [2, 8192, 5120], P('cfg', ('blk', 'uly')), may hold values from -6 to 6
- latent: float32 [8192, 5120], P(('blk', 'uly'), 'cfg'), may hold values from -6 to 6
- previous_velocity: float32 [8192, 5120], P(('blk', 'uly'), 'cfg'), may hold values from -12 to 12
Outputs:
- velocity: float32 [8192, 5120], P(('blk', 'uly'), 'cfg')
- latent_next: float32 [8192, 5120], P(('blk', 'uly'), 'cfg')
All inputs are finite; a program needn't handle non-finite values.
Results may differ from a plain program's by a relative error of at most 0.006.
Values may be sent and summed in bfloat16 or wider, within the bound.
A program may use at most 64 MiB of HBM per device.

v0:
```python
import math

import jax
import jax.numpy as jnp
from jax import lax
from jax.sharding import PartitionSpec as P

HEAD_DIM = 128


guidance_scale = 5.0
step_size = 0.25


def shifted(value, axis, steps):
    count = lax.axis_size(axis)
    pairs = [(source, (source + steps) % count) for source in range(count)]
    return lax.ppermute(value, axis, pairs)


def swapped(value, axis, apart):
    mask = 2**apart
    pairs = [(source, source ^ mask) for source in range(lax.axis_size(axis))]
    return lax.ppermute(value, axis, pairs)


def fresh(group_heads, length):
    summed = jnp.zeros((group_heads, length, HEAD_DIM), jnp.float32)
    largest = jnp.full((group_heads, length), -1e30, jnp.float32)
    totals = jnp.zeros((group_heads, length), jnp.float32)
    return (summed, largest, totals)


def absorb(running, query_block, pair):
    summed, largest, totals = running
    key_block, value_block = pair
    group_heads = query_block.shape[1] // HEAD_DIM
    query_heads = query_block.reshape(query_block.shape[0], group_heads, HEAD_DIM)
    key_heads = key_block.reshape(key_block.shape[0], group_heads, HEAD_DIM)
    value_heads = value_block.reshape(value_block.shape[0], group_heads, HEAD_DIM)
    scores = jnp.einsum("qhd,khd->hqk", query_heads, key_heads, preferred_element_type=jnp.float32)
    scores = scores * (1.0 / math.sqrt(HEAD_DIM))
    largest_new = jnp.maximum(largest, jnp.max(scores, axis=2))
    weights = jnp.exp(scores - largest_new[:, :, None])
    factor = jnp.exp(largest - largest_new)
    totals = totals * factor + jnp.sum(weights, axis=2)
    product = jnp.einsum(
        "hqk,khd->hqd",
        weights.astype(jnp.bfloat16),
        value_heads,
        preferred_element_type=jnp.float32,
    )
    summed = summed * factor[:, :, None] + product
    return (summed, largest_new, totals)


def finish(running):
    summed, largest, totals = running
    output = (summed / totals[:, :, None]).astype(jnp.bfloat16)
    return output.transpose(1, 0, 2).reshape(output.shape[1], output.shape[0] * HEAD_DIM)


def on_device(queries, keys, values, latent, previous_velocity):
    query_local, key_local, value_local = (
        lax.all_to_all(queries[0], "uly", split_axis=1, concat_axis=0, tiled=True),
        lax.all_to_all(keys[0], "uly", split_axis=1, concat_axis=0, tiled=True),
        lax.all_to_all(values[0], "uly", split_axis=1, concat_axis=0, tiled=True),
    )
    length = query_local.shape[0]
    total_heads = query_local.shape[1] // HEAD_DIM
    laps = lax.axis_size("blk") - 1

    def circle(index, carry):
        pair, running = carry
        moved = shifted((pair[0], pair[1]), "blk", 1)
        return (moved, absorb(running, query_local, pair))

    pair, running = lax.fori_loop(
        0, laps, circle, ((key_local, value_local), fresh(total_heads, length))
    )
    attended = finish(absorb(running, query_local, pair))
    gathered = lax.all_to_all(attended, "uly", split_axis=0, concat_axis=1, tiled=True)
    branch = lax.axis_index("cfg")
    columns = gathered.shape[1] // 2
    own_start = branch * columns
    own_columns = lax.dynamic_slice_in_dim(gathered, own_start, columns, 1)
    partner = swapped(gathered, "cfg", 0)
    their_columns = lax.dynamic_slice_in_dim(partner, own_start, columns, 1)
    is_first = branch == 0
    conditional = jnp.where(is_first, own_columns, their_columns).astype(jnp.float32)
    unconditional = jnp.where(is_first, their_columns, own_columns).astype(jnp.float32)
    velocity = unconditional + guidance_scale * (conditional - unconditional)
    latent_next = latent + step_size * (1.5 * velocity - 0.5 * previous_velocity)
    return (velocity, latent_next)


def solution(mesh):
    in_specs = (
        P("cfg", ("blk", "uly"), None),
        P("cfg", ("blk", "uly"), None),
        P("cfg", ("blk", "uly"), None),
        P(("blk", "uly"), "cfg"),
        P(("blk", "uly"), "cfg"),
    )
    out_specs = (P(("blk", "uly"), "cfg"), P(("blk", "uly"), "cfg"))
    return jax.shard_map(
        on_device, mesh=mesh, in_specs=in_specs, out_specs=out_specs, check_vma=False
    )
```

profile of v0, /device:TPU:1, one launch (start us, length us, event | category | flops | bytes accessed | tf_op | source)
XLA Modules:
  0.0 525.8 jit_solution(16453923907274586218)
XLA Ops:
  2.8 7.5 %all-to-all-start.2 = ((bf16[64,8,640]{2,0,1:T(8,128)(2,1)}), bf16[64,8,640]{2,0,1:T(8,128)(2,1)S(1)}, u32[]{:S(2)}, u32[]{:S(2)}) async-start(bf16[64,8,640]{2,0,1:T(8,128)(2,1)} %copy.66), calls=%async_computation.2 | async-start | bytes 1310720 | tf_op jit(solution)/shard_map/all_to_all | solution.py:65
  12.3 8.2 %all-to-all-done.2 = bf16[64,8,640]{2,0,1:T(8,128)(2,1)S(1)} async-done(((bf16[64,8,640]{2,0,1:T(8,128)(2,1)}), bf16[64,8,640]{2,0,1:T(8,128)(2,1)S(1)}, u32[]{:S(2)}, u32[]{:S(2)}) %all-to-all-start.2) | async-done | bytes 655392 | tf_op jit(solution)/shard_map/all_to_all | solution.py:65
  27.2 9.5 %all-to-all-done = bf16[64,8,640]{2,0,1:T(8,128)(2,1)S(1)} async-done(((bf16[64,8,640]{2,0,1:T(8,128)(2,1)}), bf16[64,8,640]{2,0,1:T(8,128)(2,1)S(1)}, u32[]{:S(2)}, u32[]{:S(2)}) %all-to-all-start) | async-done | bytes 655392 | tf_op jit(solution)/shard_map/all_to_all | solution.py:66
  43.5 8.4 %all-to-all-done.1 = bf16[64,8,640]{2,0,1:T(8,128)(2,1)} async-done(((bf16[64,8,640]{2,0,1:T(8,128)(2,1)}), bf16[64,8,640]{2,0,1:T(8,128)(2,1)}, u32[]{:S(2)}, u32[]{:S(2)}) %all-to-all-start.1) | async-done | bytes 655392 | tf_op jit(solution)/shard_map/all_to_all | solution.py:67
  55.7 418.9 %while.19 = (s32[]{:T(128)}, bf16[512,640]{0,1:T(8,128)(2,1)S(1)}, bf16[512,640]{0,1:T(8,128)(2,1)}, f32[5,512,128]{2,1,0:T(8,128)S(1)}, f32[5,512]{1,0:T(8,128)...) while((s32[]{:T(128)}, bf16[512,640]{0,1:T(8,128)(2,1)S(1)}, ...), condition=%wide.region_3.0_spmd.clone, body=%wide.region_0.0_spmd.clone.sunk | while | flops 682570240 | bytes 28344504 | solution.py:78
  72.9 14.1 %collective-permute-done.1 = bf16[512,640]{0,1:T(8,128)(2,1)} collective-permute-done((bf16[512,640]{0,1:T(8,128)(2,1)S(1)}, bf16[512,640]{0,1:T(8,128)(2,1)}, u32[]{:S(2)}, u32[]{:S(2)}) %collective-permute-start.1) | collective-permute-done | bytes 655392 | tf_op jit(solution)/shard_map/while/body/eval_jaxpr/ppermute | solution.py:18
  101.3 14.1 %collective-permute-done.1 = bf16[512,640]{0,1:T(8,128)(2,1)} collective-permute-done((bf16[512,640]{0,1:T(8,128)(2,1)S(1)}, bf16[512,640]{0,1:T(8,128)(2,1)}, u32[]{:S(2)}, u32[]{:S(2)}) %collective-permute-start.1) | collective-permute-done | bytes 655392 | tf_op jit(solution)/shard_map/while/body/eval_jaxpr/ppermute | solution.py:18
  128.7 14.1 %collective-permute-done.1 = bf16[512,640]{0,1:T(8,128)(2,1)} collective-permute-done((bf16[512,640]{0,1:T(8,128)(2,1)S(1)}, bf16[512,640]{0,1:T(8,128)(2,1)}, u32[]{:S(2)}, u32[]{:S(2)}) %collective-permute-start.1) | collective-permute-done | bytes 655392 | tf_op jit(solution)/shard_map/while/body/eval_jaxpr/ppermute | solution.py:18
  156.0 14.1 %collective-permute-done.1 = bf16[512,640]{0,1:T(8,128)(2,1)} collective-permute-done((bf16[512,640]{0,1:T(8,128)(2,1)S(1)}, bf16[512,640]{0,1:T(8,128)(2,1)}, u32[]{:S(2)}, u32[]{:S(2)}) %collective-permute-start.1) | collective-permute-done | bytes 655392 | tf_op jit(solution)/shard_map/while/body/eval_jaxpr/ppermute | solution.py:18
  183.3 13.9 %collective-permute-done.1 = bf16[512,640]{0,1:T(8,128)(2,1)} collective-permute-done((bf16[512,640]{0,1:T(8,128)(2,1)S(1)}, bf16[512,640]{0,1:T(8,128)(2,1)}, u32[]{:S(2)}, u32[]{:S(2)}) %collective-permute-start.1) | collective-permute-done | bytes 655392 | tf_op jit(solution)/shard_map/while/body/eval_jaxpr/ppermute | solution.py:18
  211.4 13.0 %collective-permute-done.1 = bf16[512,640]{0,1:T(8,128)(2,1)} collective-permute-done((bf16[512,640]{0,1:T(8,128)(2,1)S(1)}, bf16[512,640]{0,1:T(8,128)(2,1)}, u32[]{:S(2)}, u32[]{:S(2)}) %collective-permute-start.1) | collective-permute-done | bytes 655392 | tf_op jit(solution)/shard_map/while/body/eval_jaxpr/ppermute | solution.py:18
  239.5 12.0 %collective-permute-done.1 = bf16[512,640]{0,1:T(8,128)(2,1)} collective-permute-done((bf16[512,640]{0,1:T(8,128)(2,1)S(1)}, bf16[512,640]{0,1:T(8,128)(2,1)}, u32[]{:S(2)}, u32[]{:S(2)}) %collective-permute-start.1) | collective-permute-done | bytes 655392 | tf_op jit(solution)/shard_map/while/body/eval_jaxpr/ppermute | solution.py:18
  267.6 11.1 %collective-permute-done.1 = bf16[512,640]{0,1:T(8,128)(2,1)} collective-permute-done((bf16[512,640]{0,1:T(8,128)(2,1)S(1)}, bf16[512,640]{0,1:T(8,128)(2,1)}, u32[]{:S(2)}, u32[]{:S(2)}) %collective-permute-start.1) | collective-permute-done | bytes 655392 | tf_op jit(solution)/shard_map/while/body/eval_jaxpr/ppermute | solution.py:18
  295.6 10.1 %collective-permute-done.1 = bf16[512,640]{0,1:T(8,128)(2,1)} collective-permute-done((bf16[512,640]{0,1:T(8,128)(2,1)S(1)}, bf16[512,640]{0,1:T(8,128)(2,1)}, u32[]{:S(2)}, u32[]{:S(2)}) %collective-permute-start.1) | collective-permute-done | bytes 655392 | tf_op jit(solution)/shard_map/while/body/eval_jaxpr/ppermute | solution.py:18
  323.7 9.1 %collective-permute-done.1 = bf16[512,640]{0,1:T(8,128)(2,1)} collective-permute-done((bf16[512,640]{0,1:T(8,128)(2,1)S(1)}, bf16[512,640]{0,1:T(8,128)(2,1)}, u32[]{:S(2)}, u32[]{:S(2)}) %collective-permute-start.1) | collective-permute-done | bytes 655392 | tf_op jit(solution)/shard_map/while/body/eval_jaxpr/ppermute | solution.py:18
  345.1 6.9 %collective-permute-done = bf16[512,640]{0,1:T(8,128)(2,1)S(1)} collective-permute-done((bf16[512,640]{0,1:T(8,128)(2,1)S(1)}, bf16[512,640]{0,1:T(8,128)(2,1)S(1)}, u32[]{:S(2)}, u32[]{:S(2)}) %collective-permute-start) | collective-permute-done | bytes 655392 | tf_op jit(solution)/shard_map/while/body/eval_jaxpr/ppermute | solution.py:18
  352.0 8.0 %collective-permute-done.1 = bf16[512,640]{0,1:T(8,128)(2,1)} collective-permute-done((bf16[512,640]{0,1:T(8,128)(2,1)S(1)}, bf16[512,640]{0,1:T(8,128)(2,1)}, u32[]{:S(2)}, u32[]{:S(2)}) %collective-permute-start.1) | collective-permute-done | bytes 655392 | tf_op jit(solution)/shard_map/while/body/eval_jaxpr/ppermute | solution.py:18
  379.2 7.9 %collective-permute-done.1 = bf16[512,640]{0,1:T(8,128)(2,1)} collective-permute-done((bf16[512,640]{0,1:T(8,128)(2,1)S(1)}, bf16[512,640]{0,1:T(8,128)(2,1)}, u32[]{:S(2)}, u32[]{:S(2)}) %collective-permute-start.1) | collective-permute-done | bytes 655392 | tf_op jit(solution)/shard_map/while/body/eval_jaxpr/ppermute | solution.py:18
  406.2 8.9 %collective-permute-done.1 = bf16[512,640]{0,1:T(8,128)(2,1)} collective-permute-done((bf16[512,640]{0,1:T(8,128)(2,1)S(1)}, bf16[512,640]{0,1:T(8,128)(2,1)}, u32[]{:S(2)}, u32[]{:S(2)}) %collective-permute-start.1) | collective-permute-done | bytes 655392 | tf_op jit(solution)/shard_map/while/body/eval_jaxpr/ppermute | solution.py:18
  427.4 6.9 %collective-permute-done = bf16[512,640]{0,1:T(8,128)(2,1)S(1)} collective-permute-done((bf16[512,640]{0,1:T(8,128)(2,1)S(1)}, bf16[512,640]{0,1:T(8,128)(2,1)S(1)}, u32[]{:S(2)}, u32[]{:S(2)}) %collective-permute-start) | collective-permute-done | bytes 655392 | tf_op jit(solution)/shard_map/while/body/eval_jaxpr/ppermute | solution.py:18
  434.3 10.0 %collective-permute-done.1 = bf16[512,640]{0,1:T(8,128)(2,1)} collective-permute-done((bf16[512,640]{0,1:T(8,128)(2,1)S(1)}, bf16[512,640]{0,1:T(8,128)(2,1)}, u32[]{:S(2)}, u32[]{:S(2)}) %collective-permute-start.1) | collective-permute-done | bytes 655392 | tf_op jit(solution)/shard_map/while/body/eval_jaxpr/ppermute | solution.py:18
  463.5 11.1 %collective-permute-done.1 = bf16[512,640]{0,1:T(8,128)(2,1)} collective-permute-done((bf16[512,640]{0,1:T(8,128)(2,1)S(1)}, bf16[512,640]{0,1:T(8,128)(2,1)}, u32[]{:S(2)}, u32[]{:S(2)}) %collective-permute-start.1) | collective-permute-done | bytes 655392 | tf_op jit(solution)/shard_map/while/body/eval_jaxpr/ppermute | solution.py:18
  481.9 25.2 %all_to_all.76 = bf16[8,64,640]{2,1,0:T(8,128)(2,1)S(1)} all-to-all(bf16[8,64,640]{2,1,0:T(8,128)(2,1)S(1)} %all_to_all.68), channel_id=1, replica_groups=mesh['cfg'=2,'blk'=16,'uly'=8] {'uly'}, dimensions={0} | all-to-all | bytes 1310720 | tf_op jit(solution)/shard_map/all_to_all | solution.py:82
  507.2 15.6 %collective-permute-start.2 = (bf16[64,5120]{1,0:T(8,128)(2,1)S(1)}, bf16[64,5120]{1,0:T(8,128)(2,1)S(1)}, u32[]{:S(2)}, u32[]{:S(2)}) collective-permute-start(bf16[64,5120]{1,0:T(8,128)(2,1)S(1)} %bitcast.72), channel_id=1, source_target_pairs={{0,128},{128,0},{1,129},{129,1},{2,130},{130,2},{3,131},{131,3},{4... | collective-permute-start | bytes 1966088 | tf_op jit(solution)/shard_map/ppermute | solution.py:24
  (194 shorter events, 264.3 us)
Async XLA Ops:
  2.8 17.8 %all-to-all-start.2 = ((bf16[64,8,640]{2,0,1:T(8,128)(2,1)}), bf16[64,8,640]{2,0,1:T(8,128)(2,1)S(1)}, u32[]{:S(2)}, u32[]{:S(2)}) async-start(bf16[64,8,640]{2,0,1:T(8,128)(2,1)} %copy.66), calls=%async_computation.2 | async-start | bytes 1310720 | tf_op jit(solution)/shard_map/all_to_all | solution.py:65
  55.8 17.2 %collective-permute-start = (bf16[512,640]{0,1:T(8,128)(2,1)S(1)}, bf16[512,640]{0,1:T(8,128)(2,1)S(1)}, u32[]{:S(2)}, u32[]{:S(2)}) collective-permute-start(bf16[512,640]{0,1:T(8,128)(2,1)S(1)} %copy.98), channel_id=1, source_target_pairs={{0,8},{8,16},{16,24},{24,32},{32,40},{40,48},{48,56},{56,64},{64,7... | collective-permute-start | bytes 1966088 | tf_op jit(solution)/shard_map/while/body/eval_jaxpr/ppermute | solution.py:18
  57.3 29.8 %collective-permute-start.1 = (bf16[512,640]{0,1:T(8,128)(2,1)S(1)}, bf16[512,640]{0,1:T(8,128)(2,1)}, u32[]{:S(2)}, u32[]{:S(2)}) collective-permute-start(bf16[512,640]{0,1:T(8,128)(2,1)S(1)} %copy.99), channel_id=1, source_target_pairs={{0,8},{8,16},{16,24},{24,32},{32,40},{40,48},{48,56},{56,64},{64,7... | collective-permute-start | bytes 1966088 | tf_op jit(solution)/shard_map/while/body/eval_jaxpr/ppermute | solution.py:18
  88.3 27.1 %collective-permute-start.1 = (bf16[512,640]{0,1:T(8,128)(2,1)S(1)}, bf16[512,640]{0,1:T(8,128)(2,1)}, u32[]{:S(2)}, u32[]{:S(2)}) collective-permute-start(bf16[512,640]{0,1:T(8,128)(2,1)S(1)} %copy.99), channel_id=1, source_target_pairs={{0,8},{8,16},{16,24},{24,32},{32,40},{40,48},{48,56},{56,64},{64,7... | collective-permute-start | bytes 1966088 | tf_op jit(solution)/shard_map/while/body/eval_jaxpr/ppermute | solution.py:18
  116.7 26.2 %collective-permute-start.1 = (bf16[512,640]{0,1:T(8,128)(2,1)S(1)}, bf16[512,640]{0,1:T(8,128)(2,1)}, u32[]{:S(2)}, u32[]{:S(2)}) collective-permute-start(bf16[512,640]{0,1:T(8,128)(2,1)S(1)} %copy.99), channel_id=1, source_target_pairs={{0,8},{8,16},{16,24},{24,32},{32,40},{40,48},{48,56},{56,64},{64,7... | collective-permute-start | bytes 1966088 | tf_op jit(solution)/shard_map/while/body/eval_jaxpr/ppermute | solution.py:18
  144.1 26.0 %collective-permute-start.1 = (bf16[512,640]{0,1:T(8,128)(2,1)S(1)}, bf16[512,640]{0,1:T(8,128)(2,1)}, u32[]{:S(2)}, u32[]{:S(2)}) collective-permute-start(bf16[512,640]{0,1:T(8,128)(2,1)S(1)} %copy.99), channel_id=1, source_target_pairs={{0,8},{8,16},{16,24},{24,32},{32,40},{40,48},{48,56},{56,64},{64,7... | collective-permute-start | bytes 1966088 | tf_op jit(solution)/shard_map/while/body/eval_jaxpr/ppermute | solution.py:18
  171.3 25.9 %collective-permute-start.1 = (bf16[512,640]{0,1:T(8,128)(2,1)S(1)}, bf16[512,640]{0,1:T(8,128)(2,1)}, u32[]{:S(2)}, u32[]{:S(2)}) collective-permute-start(bf16[512,640]{0,1:T(8,128)(2,1)S(1)} %copy.99), channel_id=1, source_target_pairs={{0,8},{8,16},{16,24},{24,32},{32,40},{40,48},{48,56},{56,64},{64,7... | collective-permute-start | bytes 1966088 | tf_op jit(solution)/shard_map/while/body/eval_jaxpr/ppermute | solution.py:18
  198.5 25.9 %collective-permute-start.1 = (bf16[512,640]{0,1:T(8,128)(2,1)S(1)}, bf16[512,640]{0,1:T(8,128)(2,1)}, u32[]{:S(2)}, u32[]{:S(2)}) collective-permute-start(bf16[512,640]{0,1:T(8,128)(2,1)S(1)} %copy.99), channel_id=1, source_target_pairs={{0,8},{8,16},{16,24},{24,32},{32,40},{40,48},{48,56},{56,64},{64,7... | collective-permute-start | bytes 1966088 | tf_op jit(solution)/shard_map/while/body/eval_jaxpr/ppermute | solution.py:18
  225.6 25.9 %collective-permute-start.1 = (bf16[512,640]{0,1:T(8,128)(2,1)S(1)}, bf16[512,640]{0,1:T(8,128)(2,1)}, u32[]{:S(2)}, u32[]{:S(2)}) collective-permute-start(bf16[512,640]{0,1:T(8,128)(2,1)S(1)} %copy.99), channel_id=1, source_target_pairs={{0,8},{8,16},{16,24},{24,32},{32,40},{40,48},{48,56},{56,64},{64,7... | collective-permute-start | bytes 1966088 | tf_op jit(solution)/shard_map/while/body/eval_jaxpr/ppermute | solution.py:18
  252.7 25.9 %collective-permute-start.1 = (bf16[512,640]{0,1:T(8,128)(2,1)S(1)}, bf16[512,640]{0,1:T(8,128)(2,1)}, u32[]{:S(2)}, u32[]{:S(2)}) collective-permute-start(bf16[512,640]{0,1:T(8,128)(2,1)S(1)} %copy.99), channel_id=1, source_target_pairs={{0,8},{8,16},{16,24},{24,32},{32,40},{40,48},{48,56},{56,64},{64,7... | collective-permute-start | bytes 1966088 | tf_op jit(solution)/shard_map/while/body/eval_jaxpr/ppermute | solution.py:18
  279.9 25.9 %collective-permute-start.1 = (bf16[512,640]{0,1:T(8,128)(2,1)S(1)}, bf16[512,640]{0,1:T(8,128)(2,1)}, u32[]{:S(2)}, u32[]{:S(2)}) collective-permute-start(bf16[512,640]{0,1:T(8,128)(2,1)S(1)} %copy.99), channel_id=1, source_target_pairs={{0,8},{8,16},{16,24},{24,32},{32,40},{40,48},{48,56},{56,64},{64,7... | collective-permute-start | bytes 1966088 | tf_op jit(solution)/shard_map/while/body/eval_jaxpr/ppermute | solution.py:18
  305.8 17.9 %collective-permute-start = (bf16[512,640]{0,1:T(8,128)(2,1)S(1)}, bf16[512,640]{0,1:T(8,128)(2,1)S(1)}, u32[]{:S(2)}, u32[]{:S(2)}) collective-permute-start(bf16[512,640]{0,1:T(8,128)(2,1)S(1)} %copy.98), channel_id=1, source_target_pairs={{0,8},{8,16},{16,24},{24,32},{32,40},{40,48},{48,56},{56,64},{64,7... | collective-permute-start | bytes 1966088 | tf_op jit(solution)/shard_map/while/body/eval_jaxpr/ppermute | solution.py:18
  307.0 25.9 %collective-permute-start.1 = (bf16[512,640]{0,1:T(8,128)(2,1)S(1)}, bf16[512,640]{0,1:T(8,128)(2,1)}, u32[]{:S(2)}, u32[]{:S(2)}) collective-permute-start(bf16[512,640]{0,1:T(8,128)(2,1)S(1)} %copy.99), channel_id=1, source_target_pairs={{0,8},{8,16},{16,24},{24,32},{32,40},{40,48},{48,56},{56,64},{64,7... | collective-permute-start | bytes 1966088 | tf_op jit(solution)/shard_map/while/body/eval_jaxpr/ppermute | solution.py:18
  332.9 19.1 %collective-permute-start = (bf16[512,640]{0,1:T(8,128)(2,1)S(1)}, bf16[512,640]{0,1:T(8,128)(2,1)S(1)}, u32[]{:S(2)}, u32[]{:S(2)}) collective-permute-start(bf16[512,640]{0,1:T(8,128)(2,1)S(1)} %copy.98), channel_id=1, source_target_pairs={{0,8},{8,16},{16,24},{24,32},{32,40},{40,48},{48,56},{56,64},{64,7... | collective-permute-start | bytes 1966088 | tf_op jit(solution)/shard_map/while/body/eval_jaxpr/ppermute | solution.py:18
  334.1 25.9 %collective-permute-start.1 = (bf16[512,640]{0,1:T(8,128)(2,1)S(1)}, bf16[512,640]{0,1:T(8,128)(2,1)}, u32[]{:S(2)}, u32[]{:S(2)}) collective-permute-start(bf16[512,640]{0,1:T(8,128)(2,1)S(1)} %copy.99), channel_id=1, source_target_pairs={{0,8},{8,16},{16,24},{24,32},{32,40},{40,48},{48,56},{56,64},{64,7... | collective-permute-start | bytes 1966088 | tf_op jit(solution)/shard_map/while/body/eval_jaxpr/ppermute | solution.py:18
  360.1 19.1 %collective-permute-start = (bf16[512,640]{0,1:T(8,128)(2,1)S(1)}, bf16[512,640]{0,1:T(8,128)(2,1)S(1)}, u32[]{:S(2)}, u32[]{:S(2)}) collective-permute-start(bf16[512,640]{0,1:T(8,128)(2,1)S(1)} %copy.98), channel_id=1, source_target_pairs={{0,8},{8,16},{16,24},{24,32},{32,40},{40,48},{48,56},{56,64},{64,7... | collective-permute-start | bytes 1966088 | tf_op jit(solution)/shard_map/while/body/eval_jaxpr/ppermute | solution.py:18
  361.2 25.8 %collective-permute-start.1 = (bf16[512,640]{0,1:T(8,128)(2,1)S(1)}, bf16[512,640]{0,1:T(8,128)(2,1)}, u32[]{:S(2)}, u32[]{:S(2)}) collective-permute-start(bf16[512,640]{0,1:T(8,128)(2,1)S(1)} %copy.99), channel_id=1, source_target_pairs={{0,8},{8,16},{16,24},{24,32},{32,40},{40,48},{48,56},{56,64},{64,7... | collective-permute-start | bytes 1966088 | tf_op jit(solution)/shard_map/while/body/eval_jaxpr/ppermute | solution.py:18
  387.1 19.1 %collective-permute-start = (bf16[512,640]{0,1:T(8,128)(2,1)S(1)}, bf16[512,640]{0,1:T(8,128)(2,1)S(1)}, u32[]{:S(2)}, u32[]{:S(2)}) collective-permute-start(bf16[512,640]{0,1:T(8,128)(2,1)S(1)} %copy.98), channel_id=1, source_target_pairs={{0,8},{8,16},{16,24},{24,32},{32,40},{40,48},{48,56},{56,64},{64,7... | collective-permute-start | bytes 1966088 | tf_op jit(solution)/shard_map/while/body/eval_jaxpr/ppermute | solution.py:18
  388.3 26.9 %collective-permute-start.1 = (bf16[512,640]{0,1:T(8,128)(2,1)S(1)}, bf16[512,640]{0,1:T(8,128)(2,1)}, u32[]{:S(2)}, u32[]{:S(2)}) collective-permute-start(bf16[512,640]{0,1:T(8,128)(2,1)S(1)} %copy.99), channel_id=1, source_target_pairs={{0,8},{8,16},{16,24},{24,32},{32,40},{40,48},{48,56},{56,64},{64,7... | collective-permute-start | bytes 1966088 | tf_op jit(solution)/shard_map/while/body/eval_jaxpr/ppermute | solution.py:18
  415.2 19.1 %collective-permute-start = (bf16[512,640]{0,1:T(8,128)(2,1)S(1)}, bf16[512,640]{0,1:T(8,128)(2,1)S(1)}, u32[]{:S(2)}, u32[]{:S(2)}) collective-permute-start(bf16[512,640]{0,1:T(8,128)(2,1)S(1)} %copy.98), channel_id=1, source_target_pairs={{0,8},{8,16},{16,24},{24,32},{32,40},{40,48},{48,56},{56,64},{64,7... | collective-permute-start | bytes 1966088 | tf_op jit(solution)/shard_map/while/body/eval_jaxpr/ppermute | solution.py:18
  416.4 28.0 %collective-permute-start.1 = (bf16[512,640]{0,1:T(8,128)(2,1)S(1)}, bf16[512,640]{0,1:T(8,128)(2,1)}, u32[]{:S(2)}, u32[]{:S(2)}) collective-permute-start(bf16[512,640]{0,1:T(8,128)(2,1)S(1)} %copy.99), channel_id=1, source_target_pairs={{0,8},{8,16},{16,24},{24,32},{32,40},{40,48},{48,56},{56,64},{64,7... | collective-permute-start | bytes 1966088 | tf_op jit(solution)/shard_map/while/body/eval_jaxpr/ppermute | solution.py:18
  444.4 19.1 %collective-permute-start = (bf16[512,640]{0,1:T(8,128)(2,1)S(1)}, bf16[512,640]{0,1:T(8,128)(2,1)S(1)}, u32[]{:S(2)}, u32[]{:S(2)}) collective-permute-start(bf16[512,640]{0,1:T(8,128)(2,1)S(1)} %copy.98), channel_id=1, source_target_pairs={{0,8},{8,16},{16,24},{24,32},{32,40},{40,48},{48,56},{56,64},{64,7... | collective-permute-start | bytes 1966088 | tf_op jit(solution)/shard_map/while/body/eval_jaxpr/ppermute | solution.py:18
  445.6 29.0 %collective-permute-start.1 = (bf16[512,640]{0,1:T(8,128)(2,1)S(1)}, bf16[512,640]{0,1:T(8,128)(2,1)}, u32[]{:S(2)}, u32[]{:S(2)}) collective-permute-start(bf16[512,640]{0,1:T(8,128)(2,1)S(1)} %copy.99), channel_id=1, source_target_pairs={{0,8},{8,16},{16,24},{24,32},{32,40},{40,48},{48,56},{56,64},{64,7... | collective-permute-start | bytes 1966088 | tf_op jit(solution)/shard_map/while/body/eval_jaxpr/ppermute | solution.py:18
  507.2 17.3 %collective-permute-start.2 = (bf16[64,5120]{1,0:T(8,128)(2,1)S(1)}, bf16[64,5120]{1,0:T(8,128)(2,1)S(1)}, u32[]{:S(2)}, u32[]{:S(2)}) collective-permute-start(bf16[64,5120]{1,0:T(8,128)(2,1)S(1)} %bitcast.72), channel_id=1, source_target_pairs={{0,128},{128,0},{1,129},{129,1},{2,130},{130,2},{3,131},{131,3},{4... | collective-permute-start | bytes 1966088 | tf_op jit(solution)/shard_map/ppermute | solution.py:24
  (13 other events, 260.2 us)
where the time goes:
time: 528 us; the launch traced here: 526 us
  waiting for transfers between devices  260 us (49%)
  matrix products  119 us (23%)
  other arithmetic  52.8 us (10%)
  starting transfers between devices  38.1 us (7%)
  local copies, waits for them, and re-layouts  28.8 us (5%)
  blocking collectives  25.2 us (5%)
    ppermute x30, waiting for transfers between devices, shifted(): return lax.ppermute(value, axis, pairs)  232 us
    dot_general x16, matrix products, absorb(): jnp.einsum('qhd,khd->hqk', query_heads, key_heads, preferred_element_type...  66.4 us
    dot_general x16, matrix products, absorb(): jnp.einsum('hqk,khd->hqd', weights.astype(jnp.bfloat16), value_heads, pre...  52.7 us
    reduce_sum x16, other arithmetic, absorb(): totals = totals * factor + jnp.sum(weights, axis=2)  51.2 us
    all_to_all x1, blocking collectives, on_device(): lax.all_to_all(attended, 'uly', split_axis=0, concat_axis=1, tiled=True)  25.2 us
    while x45, local copies, waits for them, and re-layouts  17 us
    ppermute x1, starting transfers between devices, swapped(): return lax.ppermute(value, axis, pairs)  15.6 us
  transfers between devices with their start and end apart: 34, of which 34 were waited for; matrix products, arithmetic and copies ran while one was open for 35% of the time, Pallas kernels for 0%

commit v1 on v0

v1 whole, which is shorter than its diff:
```python
import functools
import math

import jax
import jax.numpy as jnp
from jax import lax
from jax.experimental import pallas as pl
from jax.experimental.pallas import tpu as pltpu
from jax.sharding import PartitionSpec as P

HEAD_DIM = 128

guidance_scale = 5.0
step_size = 0.25

EXP2_SCALE = math.log2(math.e) / math.sqrt(HEAD_DIM)
MESH = pl.DeviceIdType.MESH
LOOKAHEAD = 1


def nt(left, right):
    return lax.dot_general(
        left, right, (((1,), (1,)), ((), ())), preferred_element_type=jnp.float32
    )


def kernel(
    nz, side, rows,
    q_ref, k_ref, v_ref, out_ref,
    kv, qm, q5, vt, vt5, acc, top, acc5, top5,
    o_send, p_send, l_send, o_got, p_got, l_got, merged,
    q_sem, q5_sem, q5f_sem, kv_sem, fwd_sem, o_sem, p_sem, l_sem, out_sem,
    q_sent, kv_sent, q5f_sent, fwd_sent, o_sent, p_sent, l_sent, out_sent,
):
    heads = side + 1
    half = nz // 2
    group = half * rows
    block = nz * rows
    queries = side * block
    c = lax.axis_index("cfg")
    blk = lax.axis_index("blk")
    uly = lax.axis_index("uly")
    z = lax.div(blk, 2)
    x = lax.div(uly, side) * 2 + lax.rem(blk, 2)
    y = lax.rem(uly, side)
    a = x * (1 - c) + y * c
    b = y * (1 - c) + x * c

    def chip(x_, y_, z_, core):
        return (core, z_ * 2 + lax.rem(x_, 2), lax.div(x_, 2) * side + y_)

    def dev(a_, b_, z_, core=None):
        return chip(a_ * (1 - c) + b_ * c, b_ * (1 - c) + a_ * c, z_, c if core is None else core)

    def minus(value, steps, count):
        return lax.rem(value + count - steps, count)

    def plus(value, steps, count):
        return lax.rem(value + steps, count)

    def remote(src, dst, sent, got, device):
        return pltpu.make_async_remote_copy(
            src_ref=src, dst_ref=dst, send_sem=sent, recv_sem=got,
            device_id=device, device_id_type=MESH,
        )

    def await_bytes(ref, sem):
        pltpu.make_async_copy(ref, ref, sem).wait()

    barrier = pltpu.get_barrier_semaphore()

    def greet(device):
        pl.semaphore_signal(barrier, inc=1, device_id=device, device_id_type=MESH)

    def greet_layer(s, _):
        z_ = minus(z, s, nz)
        for r in range(side):
            greet(dev(minus(a, r, side), b, z_))
        greet(chip(x, y, z_, 1 - c))
        return 0

    for r in range(1, side):
        greet(dev(minus(a, r, side), b, z))
        greet(dev(a, minus(b, r, side), z))
        greet(chip(minus(x, r, side), y, z, 1 - c))
        greet(chip(x, minus(y, r, side), z, 1 - c))
    greet(chip(x, y, z, 1 - c))
    lax.fori_loop(1, nz, greet_layer, 0)
    pl.semaphore_wait(barrier, 4 * (side - 1) + 1 + (nz - 1) * (side + 1))

    def cols(z_, head):
        return pl.ds(pl.multiple_of((z_ * heads + head) * HEAD_DIM, HEAD_DIM), HEAD_DIM)

    def order(i):
        back = lax.rem(nz - lax.div(i, 2), nz)
        odd = lax.rem(i, 2)
        return odd * lax.div(i + 1, 2) + (1 - odd) * back

    def send_q(s, z_, first):
        for r in range(first, side):
            a_ = minus(a, r, side)
            remote(q_ref.at[0, :, cols(z_, a_)], qm.at[r, s], q_sent.at[s], q_sem,
                   dev(a_, b, z_)).start()

    def send_kv(s, z_, first):
        for r in range(first, side):
            a_ = minus(a, r, side)
            for part, ref in ((0, k_ref), (1, v_ref)):
                remote(ref.at[0, :, cols(z_, a_)], kv.at[s, part, 0, r], kv_sent.at[s],
                       kv_sem.at[s], dev(a_, b, z_)).start()

    def send_q_layer(i, _):
        s = order(i)
        z_ = minus(z, s, nz)
        remote(q_ref.at[0, :, cols(z_, side)], q5.at[0, s], q_sent.at[s], q5_sem,
               dev(a, b, z_)).start()
        send_q(s, z_, 0)
        return 0

    def send_kv_layer(i, _):
        s = order(i)
        z_ = minus(z, s, nz)
        send_kv(s, z_, 0)
        for part, ref in ((0, k_ref), (1, v_ref)):
            remote(ref.at[0, :, cols(z_, side)], kv.at[s, part, 0, side], kv_sent.at[s],
                   kv_sem.at[s], dev(a, b, z_)).start()
        return 0

    pltpu.make_async_copy(q_ref.at[0, :, cols(z, side)], q5.at[0, 0], q5_sem).start()
    pltpu.make_async_copy(q_ref.at[0, :, cols(z, a)], qm.at[0, 0], q_sem).start()
    for part, ref in ((0, k_ref), (1, v_ref)):
        pltpu.make_async_copy(ref.at[0, :, cols(z, a)], kv.at[0, part, 0, 0], kv_sem.at[0]).start()
        pltpu.make_async_copy(ref.at[0, :, cols(z, side)], kv.at[0, part, 0, side], kv_sem.at[0]).start()
    lax.fori_loop(1, nz, send_q_layer, 0)
    send_q(0, z, 1)
    send_kv(0, z, 1)
    lax.fori_loop(1, nz, send_kv_layer, 0)

    acc[...] = jnp.zeros_like(acc)
    top[...] = jnp.full_like(top, -1e30)
    acc5[...] = jnp.zeros_like(acc5)
    top5[...] = jnp.full_like(top5, -1e30)
    vt[HEAD_DIM:, :] = jnp.ones((vt.shape[0] - HEAD_DIM, vt.shape[1]), vt.dtype)
    vt5[HEAD_DIM:, :] = jnp.ones((vt5.shape[0] - HEAD_DIM, vt5.shape[1]), vt5.dtype)

    def forward(s):
        await_bytes(kv.at[s, :, 0], kv_sem.at[s])
        for r in range(1, side):
            remote(kv.at[s, :, 0], kv.at[s, :, r], fwd_sent.at[s], fwd_sem.at[s],
                   dev(a, minus(b, r, side), z)).start()

    forward(0)
    await_bytes(q5.at[0], q5_sem)
    for r in range(1, side):
        remote(q5.at[0], q5.at[r], q5f_sent, q5f_sem, dev(minus(a, r, side), b, z)).start()
    await_bytes(qm, q_sem)
    await_bytes(q5.at[pl.ds(1, side - 1)], q5f_sem)

    def absorb(keys, values_t, tiles, total, largest):
        scores = [nt(keys, tile) for tile in tiles]
        width = queries // len(tiles)
        for index, score in enumerate(scores):
            at = pl.ds(index * width, width)
            old = largest[:, at]
            new = jnp.maximum(old, jnp.max(score, axis=0, keepdims=True))
            weights = jnp.exp2((score - new) * EXP2_SCALE).astype(jnp.bfloat16)
            factor = jnp.exp2((old - new) * EXP2_SCALE)
            total[:, at] = total[:, at] * factor + jnp.dot(
                values_t, weights, preferred_element_type=jnp.float32
            )
            largest[:, at] = new

    tiles = max(1, queries // 1024)
    tile_r = side // tiles

    def step(i, _):
        s = order(i)

        @pl.when(i + LOOKAHEAD < nz)
        def _():
            forward(order(i + LOOKAHEAD))

        await_bytes(kv.at[s, :, pl.ds(1, side - 1)], fwd_sem.at[s])
        keys = kv[s, 0, :, :side].reshape(side * side * rows, HEAD_DIM)
        vt[:HEAD_DIM, :] = kv[s, 1, :, :side].reshape(side * side * rows, HEAD_DIM).T
        keys5 = kv[s, 0, :, side].reshape(side * rows, HEAD_DIM)
        vt5[:HEAD_DIM, :] = kv[s, 1, :, side].reshape(side * rows, HEAD_DIM).T
        own = [qm[t * tile_r:(t + 1) * tile_r].reshape(tile_r * block, HEAD_DIM) for t in range(tiles)]
        own5 = [q5[t * tile_r:(t + 1) * tile_r].reshape(tile_r * block, HEAD_DIM) for t in range(tiles)]
        absorb(keys, vt[...], own, acc, top)
        absorb(keys5, vt5[...], own5, acc5, top5)
        return 0

    for i in range(1, LOOKAHEAD):
        forward(order(jnp.int32(i)))
    lax.fori_loop(0, nz, step, 0)

    for r in range(side):
        a_ = plus(a, r, side)
        at = pl.ds(r * block, block)
        sums = acc5[HEAD_DIM:HEAD_DIM + 1, at]
        part = (acc5[:HEAD_DIM, at] / sums).astype(jnp.bfloat16)
        log_sum = jnp.broadcast_to(top5[:, at] * EXP2_SCALE + jnp.log2(sums), (8, block))
        for h in range(2):
            p_send[r, h] = part[:, h * group:(h + 1) * group]
            l_send[r, h] = log_sum[:, h * group:(h + 1) * group]
        own = acc[:HEAD_DIM, at] / acc[HEAD_DIM:HEAD_DIM + 1, at]
        o_send[r] = own.T.astype(jnp.bfloat16).reshape(2, group, HEAD_DIM)
        for h in range(2):
            moves = (
                (p_send.at[r, h], p_got.at[c, r], p_sent, p_sem),
                (l_send.at[r, h], l_got.at[c, r], l_sent, l_sem),
                (o_send.at[r, h], o_got.at[c, a], o_sent, o_sem),
            )

            def send():
                for src, dst, sent, got in moves:
                    remote(src, dst, sent, got, dev(a_, b, z, h)).start()

            def keep():
                for src, dst, sent, got in moves:
                    pltpu.make_async_copy(src, dst, got).start()

            if r:
                send()
            else:
                pl.when(c == h)(keep)
                pl.when(c != h)(send)

    def guided(conditional, unconditional):
        return unconditional + guidance_scale * (conditional - unconditional)

    await_bytes(p_got, p_sem)
    await_bytes(l_got, l_sem)
    joined = []
    for branch in range(2):
        log_sums = [l_got[branch, r][:1] for r in range(side)]
        largest = functools.reduce(jnp.maximum, log_sums)
        shares = [jnp.exp2(value - largest) for value in log_sums]
        total = sum(shares)
        joined.append(
            sum(p_got[branch, r].astype(jnp.float32) * (shares[r] / total) for r in range(side))
        )
    merged[:, side * HEAD_DIM:] = guided(*joined).T.astype(jnp.bfloat16)
    await_bytes(o_got, o_sem)
    for head in range(side):
        merged[:, head * HEAD_DIM:(head + 1) * HEAD_DIM] = guided(
            o_got[0, head].astype(jnp.float32), o_got[1, head].astype(jnp.float32)
        ).astype(jnp.bfloat16)

    width = heads * HEAD_DIM
    target = lax.div(z, half)
    place = out_ref.at[:, pl.ds(pl.multiple_of(lax.rem(z, half) * width, HEAD_DIM), width)]
    for j in range(half):
        s = c * half + j
        src = merged.at[pl.ds(j * rows, rows)]

        def send():
            remote(src, place, out_sent.at[j], out_sem, chip(x, y, plus(z, s, nz), target)).start()

        def keep():
            pltpu.make_async_copy(src, place, out_sem).start()

        if j:
            send()
        else:
            at_home = (c == 0) & (target == 0)
            pl.when(at_home)(keep)
            pl.when(jnp.logical_not(at_home))(send)

    await_bytes(kv.at[0, 0, 0, pl.ds(1, side - 1)], q_sent.at[0])
    await_bytes(kv.at[0, :, 0, pl.ds(1, side - 1)], kv_sent.at[0])

    def sent_layer(s, _):
        await_bytes(kv.at[s, 0, 0], q_sent.at[s])
        await_bytes(kv.at[s, :, 0], kv_sent.at[s])
        return 0

    lax.fori_loop(1, nz, sent_layer, 0)

    def sent_forward(s, _):
        await_bytes(kv.at[s, :, pl.ds(1, side - 1)], fwd_sent.at[s])
        return 0

    lax.fori_loop(0, nz, sent_forward, 0)
    await_bytes(q5.at[pl.ds(1, side - 1)], q5f_sent)
    for buffer, sem in ((p_send, p_sent), (l_send, l_sent), (o_send, o_sent)):
        await_bytes(buffer.at[pl.ds(1, side - 1)], sem)
        await_bytes(buffer.at[0, 0], sem)
    for j in range(half):
        src = merged.at[pl.ds(j * rows, rows)]
        if j:
            await_bytes(src, out_sent.at[j])
        else:
            pl.when(jnp.logical_not((c == 0) & (target == 0)))(
                lambda: await_bytes(src, out_sent.at[0])
            )
    await_bytes(out_ref, out_sem)


def on_device(queries, keys, values, latent, previous_velocity):
    nz = lax.axis_size("blk") // 2
    side = math.isqrt(lax.axis_size("uly") * 2)
    rows = queries.shape[1]
    columns = queries.shape[2] // 2
    heads = side + 1
    group = nz // 2 * rows
    count = side * nz * rows
    pad = 16
    dma = pltpu.SemaphoreType.DMA
    bf16, f32 = jnp.bfloat16, jnp.float32
    moved = pl.pallas_call(
        functools.partial(kernel, nz, side, rows),
        out_shape=jax.ShapeDtypeStruct((rows, columns), bf16),
        in_specs=[pl.BlockSpec(memory_space=pl.ANY)] * 3,
        out_specs=pl.BlockSpec(memory_space=pl.ANY),
        scratch_shapes=[
            pltpu.VMEM((nz, 2, side, heads, rows, HEAD_DIM), bf16),
            pltpu.VMEM((side, nz, rows, HEAD_DIM), bf16),
            pltpu.VMEM((side, nz, rows, HEAD_DIM), bf16),
            pltpu.VMEM((HEAD_DIM + pad, side * side * rows), bf16),
            pltpu.VMEM((HEAD_DIM + pad, side * rows), bf16),
            pltpu.VMEM((HEAD_DIM + pad, count), f32),
            pltpu.VMEM((1, count), f32),
            pltpu.VMEM((HEAD_DIM + pad, count), f32),
            pltpu.VMEM((1, count), f32),
            pltpu.VMEM((side, 2, group, HEAD_DIM), bf16),
            pltpu.VMEM((side, 2, HEAD_DIM, group), bf16),
            pltpu.VMEM((side, 2, 8, group), f32),
            pltpu.VMEM((2, side, group, HEAD_DIM), bf16),
            pltpu.VMEM((2, side, HEAD_DIM, group), bf16),
            pltpu.VMEM((2, side, 8, group), f32),
            pltpu.VMEM((group, heads * HEAD_DIM), bf16),
            dma, dma, dma, dma((nz,)), dma((nz,)), dma, dma, dma, dma,
            dma((nz,)), dma((nz,)), dma, dma((nz,)), dma, dma, dma, dma((nz // 2,)),
        ],
        compiler_params=pltpu.CompilerParams(
            collective_id=0, has_side_effects=True, vmem_limit_bytes=56 * 2**20
        ),
    )(queries, keys, values)
    velocity = moved.astype(jnp.float32)
    latent_next = latent + step_size * (1.5 * velocity - 0.5 * previous_velocity)
    return (velocity, latent_next)


def solution(mesh):
    in_specs = (
        P("cfg", ("blk", "uly"), None),
        P("cfg", ("blk", "uly"), None),
        P("cfg", ("blk", "uly"), None),
        P(("blk", "uly"), "cfg"),
        P(("blk", "uly"), "cfg"),
    )
    out_specs = (P(("blk", "uly"), "cfg"), P(("blk", "uly"), "cfg"))
    return jax.shard_map(
        on_device, mesh=mesh, in_specs=in_specs, out_specs=out_specs, check_vma=False
    )
```

time: 528 us -> 103 us (0.20)
  waiting for transfers between devices: 260 us -> 0 us
  matrix products: 119 us -> 0 us
  Pallas kernels: 0 us -> 100 us
  other arithmetic: 52.8 us -> 2.16 us
  starting transfers between devices: 38.1 us -> 0 us
  local copies, waits for them, and re-layouts: 28.8 us -> 0.01 us
  blocking collectives: 25.2 us -> 0 us
    ppermute x31 -> x0, waiting for transfers between devices: 234 us -> none  [the longest x30 232 us: shifted(): return lax.ppermute(value, axis, pairs)]
    dot_general x32 -> x0, matrix products: 119 us -> none  [the longest x16 66.4 us: absorb(): jnp.einsum('qhd,khd->hqk', query_heads, key_heads, preferred_element_type...]
    pallas_call x0 -> x1, Pallas kernels: none -> 100 us  [on_device(): pl.pallas_call(functools.partial(kernel, nz, side, rows), out_shape=jax.S...]
    reduce_sum x16 -> x0, other arithmetic: 51.2 us -> none  [absorb(): totals = totals * factor + jnp.sum(weights, axis=2)]
    all_to_all x3 -> x0, waiting for transfers between devices: 26.1 us -> none  [the longest x1 9.52 us: on_device(): lax.all_to_all(keys[0], 'uly', split_axis=1, concat_axis=0, tiled=True)]
    all_to_all x1 -> x0, blocking collectives: 25.2 us -> none  [on_device(): lax.all_to_all(attended, 'uly', split_axis=0, concat_axis=1, tiled=True)]
    ppermute x31 -> x0, starting transfers between devices: 19.7 us -> none  [the longest x1 15.6 us: swapped(): return lax.ppermute(value, axis, pairs)]
    all_to_all x3 -> x0, starting transfers between devices: 18.4 us -> none  [the longest x1 7.48 us: on_device(): lax.all_to_all(queries[0], 'uly', split_axis=1, concat_axis=0, tiled=True)]
  transfers between devices with their start and end apart: 34 -> 0, of which waited for: 34 -> 0; matrix products, arithmetic and copies ran while one was open for 35% -> 0% of each run, Pallas kernels for 0% -> 0%
where the time goes in v1:
time: 103 us
  Pallas kernels  100 us (97%)
  other arithmetic  2.16 us (2%)
    pallas_call x1, Pallas kernels, on_device(): pl.pallas_call(functools.partial(kernel, nz, side, rows), out_shape=jax.S...  100 us
    add x1, other arithmetic, on_device(): latent + step_size * (1.5 * velocity - 0.5 * previous_velocity)  2.16 us

profile of v1, /device:TPU:1, one launch (start us, length us, event | category | flops | bytes accessed | tf_op | source)
XLA Modules:
  0.0 103.0 jit_solution(2099677013335248250)
XLA Ops:
  0.6 0.0 copy-start.1
  0.6 0.0 copy-start
  0.7 100.1 %shard_map.68 = bf16[64,2560]{1,0:T(8,128)(2,1)} custom-call(bf16[1,64,5120]{2,1,0:T(8,128)(2,1)} %q_ref.1, bf16[1,64,5120]{2,1,0:T(8,128)(2,1)} %k_ref.1, bf16[1,64,5120]{2,1,0:T(8,128)(2,1)} %v_ref.1), custom_call_target="tpu_custom_call" | custom-call | tf_op jit(solution)/shard_map/pallas_call | solution.py:312
  100.8 0.0 copy-done.1
  100.8 0.0 copy-done
  100.8 2.2 %multiply_add_fusion = (f32[64,2560]{1,0:T(8,128)}, f32[64,2560]{1,0:T(8,128)}) fusion(f32[64,2560]{1,0:T(8,128)S(1)} %copy-done, f32[64,2560]{1,0:T(8,128)S(1)} %copy-done.1, bf16[64,2560]{1,0:T(8,128)(2,1)} %shard_map.68), kind=kLoop, calls=%fused_computation | loop fusion | flops 983040 | bytes 2949120 | tf_op jit(solution)/shard_map/add | solution.py:342
Async XLA Ops:
  0.6 100.2 %copy-start.1 = (f32[64,2560]{1,0:T(8,128)S(1)}, f32[64,2560]{1,0:T(8,128)}, u32[]{:S(2)}) copy-start(f32[64,2560]{1,0:T(8,128)} %param.9) | copy-start | bytes 1966084
  0.6 100.2 %copy-start = (f32[64,2560]{1,0:T(8,128)S(1)}, f32[64,2560]{1,0:T(8,128)}, u32[]{:S(2)}) copy-start(f32[64,2560]{1,0:T(8,128)} %param.8) | copy-start | bytes 1966084

commit v2 on v1

v2 whole, which is shorter than its diff:
```python
import functools
import math

import jax
import jax.numpy as jnp
from jax import lax
from jax.experimental import pallas as pl
from jax.experimental.pallas import tpu as pltpu
from jax.sharding import PartitionSpec as P

HEAD_DIM = 128

guidance_scale = 5.0
step_size = 0.25

EXP2_SCALE = math.log2(math.e) / math.sqrt(HEAD_DIM)
MESH = pl.DeviceIdType.MESH
AHEAD = 8
MERGE_AT = 2
EARLY_KV = 1
LATE = 1


def nt(left, right):
    return lax.dot_general(
        left, right, (((1,), (1,)), ((), ())), preferred_element_type=jnp.float32
    )


def kernel(
    nz, side, rows,
    q_ref, k_ref, v_ref, out_ref,
    line, kv, kv5, qm, q5, vt, vt5, acc, top, acc5, top5,
    o_send, p_send, l_send, o_got, p_got, l_got, merged,
    line_sem, q_sem, q5_sem, kv5_sem, q5f_sem, kv5f_sem, kv_sem, fwd_sem, across_sem, o_sem, p_sem, l_sem, out_sem,
    line_sent, q_sent, q5_sent, kv5_sent, q5f_sent, kv5f_sent, kv_sent, fwd_sent, across_sent,
    o_sent, p_sent, l_sent, out_sent, out5_sent,
):
    heads = side + 1
    half = nz // 2
    group = half * rows
    block = nz * rows
    queries = side * block
    tiles = (0, 1, 3, 2) if half == 4 else tuple(range(half))
    early, late = tiles[:half - LATE], tiles[half - LATE:]
    c = lax.axis_index("cfg")
    blk = lax.axis_index("blk")
    uly = lax.axis_index("uly")
    z = lax.div(blk, 2)
    x = lax.div(uly, side) * 2 + lax.rem(blk, 2)
    y = lax.rem(uly, side)
    a = x * (1 - c) + y * c
    b = y * (1 - c) + x * c

    def chip(x_, y_, z_, core):
        return (core, z_ * 2 + lax.rem(x_, 2), lax.div(x_, 2) * side + y_)

    def dev(a_, b_, z_, core=None):
        return chip(a_ * (1 - c) + b_ * c, b_ * (1 - c) + a_ * c, z_, c if core is None else core)

    def minus(value, steps, count):
        return lax.rem(value + count - steps, count)

    def plus(value, steps, count):
        return lax.rem(value + steps, count)

    def remote(src, dst, sent, got, device):
        return pltpu.make_async_remote_copy(
            src_ref=src, dst_ref=dst, send_sem=sent, recv_sem=got,
            device_id=device, device_id_type=MESH,
        )

    def await_bytes(ref, sem):
        pltpu.make_async_copy(ref, ref, sem).wait()

    barrier = pltpu.get_barrier_semaphore()

    def greet(device):
        pl.semaphore_signal(barrier, inc=1, device_id=device, device_id_type=MESH)

    def greet_layer(s, _):
        z_ = minus(z, s, nz)
        for r in range(side):
            greet(dev(minus(a, r, side), b, z_))
        greet(chip(x, y, z_, 1 - c))
        return 0

    for r in range(1, side):
        greet(dev(minus(a, r, side), b, z))
        greet(dev(a, minus(b, r, side), z))
        greet(chip(minus(x, r, side), y, z, 1 - c))
        greet(chip(x, minus(y, r, side), z, 1 - c))
    greet(chip(x, y, z, 1 - c))
    lax.fori_loop(1, nz, greet_layer, 0)
    pl.semaphore_wait(barrier, 4 * (side - 1) + 1 + (nz - 1) * (side + 1))

    others = pl.ds(1, side - 1)

    def cols(z_, head):
        return pl.ds(pl.multiple_of((z_ * heads + head) * HEAD_DIM, HEAD_DIM), HEAD_DIM)

    def order(i):
        odd = lax.rem(i, 2)
        later = lax.div(i, 2) + half * jnp.minimum(i, 1)
        return odd * lax.div(i + 1, 2) + (1 - odd) * later

    shared = (
        (q_ref, lambda s: q5.at[0, s], q5_sent, q5_sem),
        (k_ref, lambda s: kv5.at[0, 0, s], kv5_sent, kv5_sem),
        (v_ref, lambda s: kv5.at[1, 0, s], kv5_sent, kv5_sem),
    )

    def send_shared(i, _):
        s = order(i)
        z_ = minus(z, s, nz)
        for ref, place, sent, got in shared:
            remote(ref.at[0, :, cols(z_, side)], place(s), sent, got, dev(a, b, z_)).start()
        return 0

    def gather_line(part, s):
        ref = (q_ref, k_ref, v_ref)[part]
        z_ = minus(z, s, nz)
        first = isinstance(s, int) and s == 0
        if first:
            place = qm.at[0, 0] if part == 0 else kv.at[0, part - 1, 0]
            got = q_sem.at[0] if part == 0 else kv_sem.at[0]
        else:
            place = line.at[part, s]
            got = line_sem.at[part, s]
        pltpu.make_async_copy(ref.at[0, :, cols(z_, a)], place.at[0], got).start()
        for r in range(1, side):
            a_ = minus(a, r, side)
            remote(ref.at[0, :, cols(z_, a_)], place.at[r], line_sent.at[part], got,
                   dev(a_, b, z)).start()

    def gather_q(i, _):
        gather_line(0, order(i))
        return 0

    def gather_kv(i, _):
        gather_line(1, order(i))
        gather_line(2, order(i))
        return 0

    def send_q(t):
        for h in range(2):
            s = t + h * half
            if s:
                await_bytes(line.at[0, s], line_sem.at[0, s])
                remote(line.at[0, s], qm.at[t, h], q_sent.at[t, h], q_sem.at[t],
                       dev(a, b, minus(z, s, nz))).start()

    def sent_q(t):
        for h in range(2):
            if t or h:
                await_bytes(qm.at[t, h], q_sent.at[t, h])

    def send_kv(s):
        for part in range(2):
            await_bytes(line.at[part + 1, s], line_sem.at[part + 1, s])
            remote(line.at[part + 1, s], kv.at[s, part, 0], kv_sent.at[s], kv_sem.at[s],
                   dev(a, b, minus(z, s, nz))).start()

    def send_kv_layer(i, _):
        send_kv(order(i))
        return 0

    near = sorted({1, side - 1})
    across = side == 4

    def forward(s):
        await_bytes(kv.at[s, :, 0], kv_sem.at[s])
        for index, r in enumerate(near):
            remote(kv.at[s, :, 0], kv.at[s, :, r], fwd_sent.at[s, index], fwd_sem.at[s, index],
                   dev(a, minus(b, r, side), z)).start()

    def relay(s):
        for index, r in enumerate(near):
            await_bytes(kv.at[s, :, r], fwd_sem.at[s, index])
            if across:
                remote(kv.at[s, index, r], kv.at[s, index, 2], across_sent.at[s], across_sem.at[s],
                       dev(a, minus(b, r, side), z)).start()

    for ref, place, sent, got in shared:
        pltpu.make_async_copy(ref.at[0, :, cols(z, side)], place(0), got).start()
    lax.fori_loop(1, nz, send_shared, 0)
    gather_line(0, 0)
    lax.fori_loop(1, nz, gather_q, 0)
    gather_line(1, 0)
    gather_line(2, 0)
    lax.fori_loop(1, nz, gather_kv, 0)

    acc[...] = jnp.zeros_like(acc)
    top[...] = jnp.full_like(top, -1e30)
    acc5[...] = jnp.zeros_like(acc5)
    top5[...] = jnp.full_like(top5, -1e30)
    vt5[HEAD_DIM:, :] = jnp.ones((vt5.shape[0] - HEAD_DIM, vt5.shape[1]), vt5.dtype)
    for s in range(nz):
        vt[s, HEAD_DIM:, :] = jnp.ones((vt.shape[1] - HEAD_DIM, vt.shape[2]), vt.dtype)

    layers = pl.ds(1, nz - 1)
    await_bytes(q5.at[0, layers], q5_sent)
    await_bytes(kv5.at[:, 0, layers], kv5_sent)
    for t in early:
        send_q(t)

    await_bytes(q5.at[0], q5_sem)
    for r in range(1, side):
        remote(q5.at[0], q5.at[r], q5f_sent, q5f_sem, dev(minus(a, r, side), b, z)).start()
    await_bytes(kv5.at[:, 0], kv5_sem)
    for r in range(1, side):
        remote(kv5.at[:, 0], kv5.at[:, r], kv5f_sent, kv5f_sem, dev(a, minus(b, r, side), z)).start()

    lax.fori_loop(1, min(EARLY_KV, nz), send_kv_layer, 0)
    for t in early:
        sent_q(t)
    lax.fori_loop(min(EARLY_KV, nz), min(AHEAD, nz), send_kv_layer, 0)

    def weigh(score, peak):
        return jnp.exp2((score - peak) * EXP2_SCALE).astype(jnp.bfloat16)

    def absorb(keys, values_t, parts, wide, rows_ref, total, largest, then=None):
        scores = [nt(keys, rows_ref[t].reshape(wide, HEAD_DIM)) for t in parts]
        for t, score in zip(parts, scores):
            at = pl.ds(t * wide, wide)
            old = largest[:, at]
            new = jnp.maximum(old, jnp.max(score, axis=0, keepdims=True))
            factor = jnp.exp2((old - new) * EXP2_SCALE)
            total[:, at] = total[:, at] * factor + jnp.dot(
                values_t[...], weigh(score, new), preferred_element_type=jnp.float32
            )
            largest[:, at] = new
            if then is not None:
                then(t, total[:, at])

    span = side * side * rows
    tile = 2 * side * rows
    chunks = nz // side
    split = side // chunks

    def absorb_shared(i, _):
        at = pl.ds(i * split, split)
        vt5[:HEAD_DIM, :] = kv5[1, at].reshape(span, HEAD_DIM).T
        absorb(kv5[0, at].reshape(span, HEAD_DIM), vt5, range(side), block, q5, acc5, top5)
        return 0

    await_bytes(q5.at[others], q5f_sem)
    await_bytes(kv5.at[:, others], kv5f_sem)
    forward(0)
    absorb_shared(0, 0)
    forward(order(jnp.int32(1)))
    relay(0)
    lax.fori_loop(1, chunks, absorb_shared, 0)

    def spread(r, moves):
        for h in range(2):
            def send():
                for src, dst, sent, got in moves(h):
                    remote(src, dst, sent, got, dev(plus(a, r, side), b, z, h)).start()

            def keep():
                for src, dst, sent, got in moves(h):
                    pltpu.make_async_copy(src, dst, got).start()

            if r:
                send()
            else:
                pl.when(c == h)(keep)
                pl.when(c != h)(send)

    for r in range(side):
        at = pl.ds(r * block, block)
        sums = acc5[HEAD_DIM:HEAD_DIM + 1, at]
        part = (acc5[:HEAD_DIM, at] / sums).astype(jnp.bfloat16)
        log_sum = jnp.broadcast_to(top5[:, at] * EXP2_SCALE + jnp.log2(sums), (8, block))
        for h in range(2):
            p_send[r, h] = part[:, h * group:(h + 1) * group]
            l_send[r, h] = log_sum[:, h * group:(h + 1) * group]
        spread(r, lambda h: (
            (p_send.at[r, h], p_got.at[c, r], p_sent, p_sem),
            (l_send.at[r, h], l_got.at[c, r], l_sent, l_sem),
        ))

    def guided(conditional, unconditional):
        return unconditional + guidance_scale * (conditional - unconditional)

    width = heads * HEAD_DIM
    target = lax.div(z, half)
    at_home = (c == 0) & (target == 0)

    def deliver(first, count, sent, *slots):
        start = pl.multiple_of(lax.rem(z, half) * width + first * HEAD_DIM, HEAD_DIM)
        place = out_ref.at[:, pl.ds(start, count * HEAD_DIM)]
        for j in slots or range(half):
            src = merged.at[pl.ds(j * rows, rows), pl.ds(first * HEAD_DIM, count * HEAD_DIM)]

            def send():
                remote(src, place, sent.at[j], out_sem,
                       chip(x, y, plus(z, c * half + j, nz), target)).start()

            def keep():
                pltpu.make_async_copy(src, place, out_sem).start()

            if j:
                send()
            else:
                pl.when(at_home)(keep)
                pl.when(jnp.logical_not(at_home))(send)

    def delivered(first, count, sent):
        for j in range(half):
            src = merged.at[pl.ds(j * rows, rows), pl.ds(first * HEAD_DIM, count * HEAD_DIM)]
            if j:
                await_bytes(src, sent.at[j])
            else:
                pl.when(jnp.logical_not(at_home))(lambda: await_bytes(src, sent.at[0]))

    def merge_shared():
        await_bytes(p_got, p_sem)
        await_bytes(l_got, l_sem)
        joined = []
        for branch in range(2):
            log_sums = [l_got[branch, r][:1] for r in range(side)]
            largest = functools.reduce(jnp.maximum, log_sums)
            shares = [jnp.exp2(value - largest) for value in log_sums]
            total = sum(shares)
            joined.append(
                sum(p_got[branch, r].astype(jnp.float32) * (shares[r] / total) for r in range(side))
            )
        merged[:, side * HEAD_DIM:] = guided(*joined).T.astype(jnp.bfloat16)
        deliver(side, 1, out5_sent)

    for t in early:
        await_bytes(qm.at[t], q_sem.at[t])

    def step(i, then):
        s = order(i)
        await_bytes(kv.at[s, :, 2], across_sem.at[s]) if across else None
        vt[s, :HEAD_DIM, :] = kv[s, 1].reshape(span, HEAD_DIM).T
        absorb(kv[s, 0].reshape(span, HEAD_DIM), vt.at[s], early, tile, qm, acc, top, then)

    def prepared_step(i, _):
        @pl.when(i + AHEAD < nz)
        def _():
            send_kv_layer(i + AHEAD, 0)

        @pl.when(i == max(nz - AHEAD, 0))
        def _():
            for t in late:
                send_q(t)

        @pl.when(i + 2 < nz)
        def _():
            forward(order(i + 2))

        relay(order(i + 1))
        pl.when(i == MERGE_AT)(merge_shared)
        step(i, None)
        return 0

    def finish(t, total):
        own = (total[:HEAD_DIM] / total[HEAD_DIM:HEAD_DIM + 1]).T
        o_send[t] = own.astype(jnp.bfloat16).reshape(2, side, rows, HEAD_DIM)
        for r in range(side):
            spread(r, lambda h: ((o_send.at[t, h, r], o_got.at[t, c, a], o_sent.at[t], o_sem.at[t]),))

    def merge(t):
        await_bytes(o_got.at[t], o_sem.at[t])
        for head in range(side):
            merged[t * rows:(t + 1) * rows, head * HEAD_DIM:(head + 1) * HEAD_DIM] = guided(
                o_got[t, 0, head].astype(jnp.float32), o_got[t, 1, head].astype(jnp.float32)
            ).astype(jnp.bfloat16)
        deliver(0, side, out_sent, t)

    lax.fori_loop(0, nz - 1, prepared_step, 0)
    step(jnp.int32(nz - 1), finish)

    def attend(t):
        own = qm[t].reshape(tile, HEAD_DIM)

        def score(s):
            return nt(kv[s, 0].reshape(span, HEAD_DIM), own)

        pairs = [(s, s + 1) for s in range(0, nz, 2)]
        ready = [score(s) for s in pairs[0]]
        peak = jnp.full((1, tile), -1e30, jnp.float32)
        total = jnp.zeros((vt.shape[1], tile), jnp.float32)
        for index, pair in enumerate(pairs):
            following = [score(s) for s in pairs[index + 1]] if index + 1 < len(pairs) else None
            new = peak
            for value in ready:
                new = jnp.maximum(new, jnp.max(value, axis=0, keepdims=True))
            total = total * jnp.exp2((peak - new) * EXP2_SCALE)
            for s, value in zip(pair, ready):
                total = total + jnp.dot(vt[s], weigh(value, new), preferred_element_type=jnp.float32)
            peak, ready = new, following
        finish(t, total)

    waiting = list(early)
    for t in late:
        await_bytes(qm.at[t], q_sem.at[t])
        attend(t)
        for done in waiting:
            merge(done)
        waiting = [t]
    for done in waiting:
        merge(done)

    for part in range(3):
        await_bytes(line.at[part, :, others], line_sent.at[part])

    def sent_layer(s, _):
        await_bytes(kv.at[s, :, 0], kv_sent.at[s])
        return 0

    lax.fori_loop(1, nz, sent_layer, 0)

    def sent_forward(s, _):
        for index, r in enumerate(near):
            await_bytes(kv.at[s, :, r], fwd_sent.at[s, index])
        if across:
            await_bytes(kv.at[s, :, 2], across_sent.at[s])
        return 0

    lax.fori_loop(0, nz, sent_forward, 0)
    await_bytes(q5.at[others], q5f_sent)
    await_bytes(kv5.at[:, others], kv5f_sent)
    for buffer, sem in ((p_send, p_sent), (l_send, l_sent)):
        await_bytes(buffer.at[others], sem)
        await_bytes(buffer.at[0, 0], sem)
    for t in range(half):
        await_bytes(o_send.at[t, :, others], o_sent.at[t])
        await_bytes(o_send.at[t, 0, 0], o_sent.at[t])
    for t in late:
        sent_q(t)
    delivered(side, 1, out5_sent)
    delivered(0, side, out_sent)
    await_bytes(out_ref, out_sem)


def on_device(queries, keys, values, latent, previous_velocity):
    nz = lax.axis_size("blk") // 2
    side = math.isqrt(lax.axis_size("uly") * 2)
    rows = queries.shape[1]
    columns = queries.shape[2] // 2
    heads = side + 1
    group = nz // 2 * rows
    count = side * nz * rows
    pad = 16
    dma = pltpu.SemaphoreType.DMA
    bf16, f32 = jnp.bfloat16, jnp.float32
    moved = pl.pallas_call(
        functools.partial(kernel, nz, side, rows),
        out_shape=jax.ShapeDtypeStruct((rows, columns), bf16),
        in_specs=[pl.BlockSpec(memory_space=pl.ANY)] * 3,
        out_specs=pl.BlockSpec(memory_space=pl.ANY),
        scratch_shapes=[
            pltpu.VMEM((3, nz, side, rows, HEAD_DIM), bf16),
            pltpu.VMEM((nz, 2, side, side, rows, HEAD_DIM), bf16),
            pltpu.VMEM((2, side, nz, rows, HEAD_DIM), bf16),
            pltpu.VMEM((nz // 2, 2, side, rows, HEAD_DIM), bf16),
            pltpu.VMEM((side, nz, rows, HEAD_DIM), bf16),
            pltpu.VMEM((nz, HEAD_DIM + pad, side * side * rows), bf16),
            pltpu.VMEM((HEAD_DIM + pad, side * side * rows), bf16),
            pltpu.VMEM((HEAD_DIM + pad, count), f32),
            pltpu.VMEM((1, count), f32),
            pltpu.VMEM((HEAD_DIM + pad, count), f32),
            pltpu.VMEM((1, count), f32),
            pltpu.VMEM((nz // 2, 2, side, rows, HEAD_DIM), bf16),
            pltpu.VMEM((side, 2, HEAD_DIM, group), bf16),
            pltpu.VMEM((side, 2, 8, group), f32),
            pltpu.VMEM((nz // 2, 2, side, rows, HEAD_DIM), bf16),
            pltpu.VMEM((2, side, HEAD_DIM, group), bf16),
            pltpu.VMEM((2, side, 8, group), f32),
            pltpu.VMEM((group, heads * HEAD_DIM), bf16),
            dma((3, nz)), dma((nz // 2,)), dma, dma, dma, dma, dma((nz,)), dma((nz, 2)), dma((nz,)),
            dma((nz // 2,)), dma, dma, dma,
            dma((3,)), dma((nz // 2, 2)), dma, dma, dma, dma, dma((nz,)), dma((nz, 2)), dma((nz,)),
            dma((nz // 2,)), dma, dma, dma((nz // 2,)), dma((nz // 2,)),
        ],
        compiler_params=pltpu.CompilerParams(
            collective_id=0, has_side_effects=True, vmem_limit_bytes=56 * 2**20
        ),
    )(queries, keys, values)
    velocity = moved.astype(jnp.float32)
    latent_next = latent + step_size * (1.5 * velocity - 0.5 * previous_velocity)
    return (velocity, latent_next)


def solution(mesh):
    in_specs = (
        P("cfg", ("blk", "uly"), None),
        P("cfg", ("blk", "uly"), None),
        P("cfg", ("blk", "uly"), None),
        P(("blk", "uly"), "cfg"),
        P(("blk", "uly"), "cfg"),
    )
    out_specs = (P(("blk", "uly"), "cfg"), P(("blk", "uly"), "cfg"))
    return jax.shard_map(
        on_device, mesh=mesh, in_specs=in_specs, out_specs=out_specs, check_vma=False
    )
```

time: 103 us -> 91.7 us (0.89)
  Pallas kernels: 100 us -> 88.7 us
    pallas_call x1, Pallas kernels: 100 us -> 88.7 us  [on_device(): pl.pallas_call(functools.partial(kernel, nz, side, rows), out_shape=jax.S...]
where the time goes in v2:
time: 91.7 us; the launch traced here: 91.6 us
  Pallas kernels  88.7 us (97%)
  other arithmetic  2.16 us (2%)
    pallas_call x1, Pallas kernels, on_device(): pl.pallas_call(functools.partial(kernel, nz, side, rows), out_shape=jax.S...  88.7 us
    add x1, other arithmetic, on_device(): latent + step_size * (1.5 * velocity - 0.5 * previous_velocity)  2.16 us

profile of v2, /device:TPU:1, one launch (start us, length us, event | category | flops | bytes accessed | tf_op | source)
XLA Modules:
  0.0 91.6 jit_solution(11787291989640972443)
XLA Ops:
  0.6 0.0 copy-start.1
  0.6 0.0 copy-start
  0.7 88.7 %shard_map.68 = bf16[64,2560]{1,0:T(8,128)(2,1)} custom-call(bf16[1,64,5120]{2,1,0:T(8,128)(2,1)} %q_ref.1, bf16[1,64,5120]{2,1,0:T(8,128)(2,1)} %k_ref.1, bf16[1,64,5120]{2,1,0:T(8,128)(2,1)} %v_ref.1), custom_call_target="tpu_custom_call" | custom-call | tf_op jit(solution)/shard_map/pallas_call | solution.py:452
  89.4 0.0 copy-done.1
  89.4 0.0 copy-done
  89.4 2.2 %multiply_add_fusion = (f32[64,2560]{1,0:T(8,128)}, f32[64,2560]{1,0:T(8,128)}) fusion(f32[64,2560]{1,0:T(8,128)S(1)} %copy-done, f32[64,2560]{1,0:T(8,128)S(1)} %copy-done.1, bf16[64,2560]{1,0:T(8,128)(2,1)} %shard_map.68), kind=kLoop, calls=%fused_computation | loop fusion | flops 983040 | bytes 2949120 | tf_op jit(solution)/shard_map/add | solution.py:486
Async XLA Ops:
  0.6 88.8 %copy-start.1 = (f32[64,2560]{1,0:T(8,128)S(1)}, f32[64,2560]{1,0:T(8,128)}, u32[]{:S(2)}) copy-start(f32[64,2560]{1,0:T(8,128)} %param.9) | copy-start | bytes 1966084
  0.6 88.8 %copy-start = (f32[64,2560]{1,0:T(8,128)S(1)}, f32[64,2560]{1,0:T(8,128)}, u32[]{:S(2)}) copy-start(f32[64,2560]{1,0:T(8,128)} %param.8) | copy-start | bytes 1966084

commit v3 on v2

--- a/solution.py
+++ b/solution.py
@@ -15,10 +15,10 @@
 
 EXP2_SCALE = math.log2(math.e) / math.sqrt(HEAD_DIM)
 MESH = pl.DeviceIdType.MESH
-AHEAD = 8
-MERGE_AT = 2
-EARLY_KV = 1
+MERGE_AT = 5
 LATE = 1
+CATCH_UP = 2
+BEFORE = 4
 
 
 def nt(left, right):
@@ -32,8 +32,8 @@
     q_ref, k_ref, v_ref, out_ref,
     line, kv, kv5, qm, q5, vt, vt5, acc, top, acc5, top5,
     o_send, p_send, l_send, o_got, p_got, l_got, merged,
-    line_sem, q_sem, q5_sem, kv5_sem, q5f_sem, kv5f_sem, kv_sem, fwd_sem, across_sem, o_sem, p_sem, l_sem, out_sem,
-    line_sent, q_sent, q5_sent, kv5_sent, q5f_sent, kv5f_sent, kv_sent, fwd_sent, across_sent,
+    line_sem, q_sem, q5_sem, kv5_sem, q5f_sem, kv5f_sem, kv_sem, fwd_sem, o_sem, p_sem, l_sem, out_sem,
+    line_sent, q_sent, q5_sent, kv5_sent, q5f_sent, kv5f_sent, kv_sent, fwd_sent,
     o_sent, p_sent, l_sent, out_sent, out5_sent,
 ):
     heads = side + 1
@@ -165,21 +165,11 @@
         send_kv(order(i))
         return 0
 
-    near = sorted({1, side - 1})
-    across = side == 4
-
     def forward(s):
         await_bytes(kv.at[s, :, 0], kv_sem.at[s])
-        for index, r in enumerate(near):
-            remote(kv.at[s, :, 0], kv.at[s, :, r], fwd_sent.at[s, index], fwd_sem.at[s, index],
+        for r in (2, 1, 3)[:side - 1] if side > 2 else (1,):
+            remote(kv.at[s, :, 0], kv.at[s, :, r], fwd_sent.at[s], fwd_sem.at[s],
                    dev(a, minus(b, r, side), z)).start()
-
-    def relay(s):
-        for index, r in enumerate(near):
-            await_bytes(kv.at[s, :, r], fwd_sem.at[s, index])
-            if across:
-                remote(kv.at[s, index, r], kv.at[s, index, 2], across_sent.at[s], across_sem.at[s],
-                       dev(a, minus(b, r, side), z)).start()
 
     for ref, place, sent, got in shared:
         pltpu.make_async_copy(ref.at[0, :, cols(z, side)], place(0), got).start()
@@ -211,10 +201,12 @@
     for r in range(1, side):
         remote(kv5.at[:, 0], kv5.at[:, r], kv5f_sent, kv5f_sem, dev(a, minus(b, r, side), z)).start()
 
-    lax.fori_loop(1, min(EARLY_KV, nz), send_kv_layer, 0)
     for t in early:
         sent_q(t)
-    lax.fori_loop(min(EARLY_KV, nz), min(AHEAD, nz), send_kv_layer, 0)
+    lax.fori_loop(1, min(1 + BEFORE, nz), send_kv_layer, 0)
+    for t in late:
+        send_q(t)
+    lax.fori_loop(min(1 + BEFORE, nz), nz, send_kv_layer, 0)
 
     def weigh(score, peak):
         return jnp.exp2((score - peak) * EXP2_SCALE).astype(jnp.bfloat16)
@@ -248,8 +240,6 @@
     await_bytes(kv5.at[:, others], kv5f_sem)
     forward(0)
     absorb_shared(0, 0)
-    forward(order(jnp.int32(1)))
-    relay(0)
     lax.fori_loop(1, chunks, absorb_shared, 0)
 
     def spread(r, moves):
@@ -335,27 +325,21 @@
 
     def step(i, then):
         s = order(i)
-        await_bytes(kv.at[s, :, 2], across_sem.at[s]) if across else None
+        await_bytes(kv.at[s, :, others], fwd_sem.at[s])
         vt[s, :HEAD_DIM, :] = kv[s, 1].reshape(span, HEAD_DIM).T
         absorb(kv[s, 0].reshape(span, HEAD_DIM), vt.at[s], early, tile, qm, acc, top, then)
 
     def prepared_step(i, _):
-        @pl.when(i + AHEAD < nz)
-        def _():
-            send_kv_layer(i + AHEAD, 0)
-
-        @pl.when(i == max(nz - AHEAD, 0))
+        forward(order(i + 1))
+        pl.when(i == MERGE_AT)(merge_shared)
+        step(i, None)
+
+        @pl.when(i == nz - CATCH_UP)
         def _():
             for t in late:
-                send_q(t)
-
-        @pl.when(i + 2 < nz)
-        def _():
-            forward(order(i + 2))
-
-        relay(order(i + 1))
-        pl.when(i == MERGE_AT)(merge_shared)
-        step(i, None)
+                await_bytes(qm.at[t], q_sem.at[t])
+                attend(t, 0, half, False)
+
         return 0
 
     def finish(t, total):
@@ -372,19 +356,19 @@
             ).astype(jnp.bfloat16)
         deliver(0, side, out_sent, t)
 
-    lax.fori_loop(0, nz - 1, prepared_step, 0)
-    step(jnp.int32(nz - 1), finish)
-
-    def attend(t):
+
+    sequence = [0] + [(i + 1) // 2 if i % 2 else i // 2 + half for i in range(1, nz)]
+
+    def attend(t, first, stop, last):
+        at = pl.ds(t * tile, tile)
         own = qm[t].reshape(tile, HEAD_DIM)
 
         def score(s):
             return nt(kv[s, 0].reshape(span, HEAD_DIM), own)
 
-        pairs = [(s, s + 1) for s in range(0, nz, 2)]
+        pairs = [sequence[i:i + 2] for i in range(first, stop, 2)]
         ready = [score(s) for s in pairs[0]]
-        peak = jnp.full((1, tile), -1e30, jnp.float32)
-        total = jnp.zeros((vt.shape[1], tile), jnp.float32)
+        peak, total = top[:, at], acc[:, at]
         for index, pair in enumerate(pairs):
             following = [score(s) for s in pairs[index + 1]] if index + 1 < len(pairs) else None
             new = peak
@@ -394,12 +378,17 @@
             for s, value in zip(pair, ready):
                 total = total + jnp.dot(vt[s], weigh(value, new), preferred_element_type=jnp.float32)
             peak, ready = new, following
-        finish(t, total)
+        if last:
+            finish(t, total)
+        else:
+            acc[:, at], top[:, at] = total, peak
+
+    lax.fori_loop(0, nz - 1, prepared_step, 0)
+    step(jnp.int32(nz - 1), finish)
 
     waiting = list(early)
     for t in late:
-        await_bytes(qm.at[t], q_sem.at[t])
-        attend(t)
+        attend(t, half, nz, True)
         for done in waiting:
             merge(done)
         waiting = [t]
@@ -416,10 +405,7 @@
     lax.fori_loop(1, nz, sent_layer, 0)
 
     def sent_forward(s, _):
-        for index, r in enumerate(near):
-            await_bytes(kv.at[s, :, r], fwd_sent.at[s, index])
-        if across:
-            await_bytes(kv.at[s, :, 2], across_sent.at[s])
+        await_bytes(kv.at[s, :, others], fwd_sent.at[s])
         return 0
 
     lax.fori_loop(0, nz, sent_forward, 0)
@@ -473,9 +459,9 @@
             pltpu.VMEM((2, side, HEAD_DIM, group), bf16),
             pltpu.VMEM((2, side, 8, group), f32),
             pltpu.VMEM((group, heads * HEAD_DIM), bf16),
-            dma((3, nz)), dma((nz // 2,)), dma, dma, dma, dma, dma((nz,)), dma((nz, 2)), dma((nz,)),
+            dma((3, nz)), dma((nz // 2,)), dma, dma, dma, dma, dma((nz,)), dma((nz,)),
             dma((nz // 2,)), dma, dma, dma,
-            dma((3,)), dma((nz // 2, 2)), dma, dma, dma, dma, dma((nz,)), dma((nz, 2)), dma((nz,)),
+            dma((3,)), dma((nz // 2, 2)), dma, dma, dma, dma, dma((nz,)), dma((nz,)),
             dma((nz // 2,)), dma, dma, dma((nz // 2,)), dma((nz // 2,)),
         ],
         compiler_params=pltpu.CompilerParams(

time: 91.7 us -> 90.8 us (level)
  no operation moved by 1% of the time
where the time goes in v3:
time: 90.8 us; the launch traced here: 90.7 us
  Pallas kernels  87.8 us (97%)
  other arithmetic  2.16 us (2%)
    pallas_call x1, Pallas kernels, on_device(): pl.pallas_call(functools.partial(kernel, nz, side, rows), out_shape=jax.S...  87.8 us
    add x1, other arithmetic, on_device(): latent + step_size * (1.5 * velocity - 0.5 * previous_velocity)  2.16 us

profile of v3, /device:TPU:1, one launch (start us, length us, event | category | flops | bytes accessed | tf_op | source)
XLA Modules:
  0.0 90.7 jit_solution(16213059669900052788)
XLA Ops:
  0.6 0.0 copy-start.1
  0.6 0.0 copy-start
  0.7 87.8 %shard_map.68 = bf16[64,2560]{1,0:T(8,128)(2,1)} custom-call(bf16[1,64,5120]{2,1,0:T(8,128)(2,1)} %q_ref.1, bf16[1,64,5120]{2,1,0:T(8,128)(2,1)} %k_ref.1, bf16[1,64,5120]{2,1,0:T(8,128)(2,1)} %v_ref.1), custom_call_target="tpu_custom_call" | custom-call | tf_op jit(solution)/shard_map/pallas_call | solution.py:438
  88.5 0.0 copy-done.1
  88.5 0.0 copy-done
  88.5 2.2 %multiply_add_fusion = (f32[64,2560]{1,0:T(8,128)}, f32[64,2560]{1,0:T(8,128)}) fusion(f32[64,2560]{1,0:T(8,128)S(1)} %copy-done, f32[64,2560]{1,0:T(8,128)S(1)} %copy-done.1, bf16[64,2560]{1,0:T(8,128)(2,1)} %shard_map.68), kind=kLoop, calls=%fused_computation | loop fusion | flops 983040 | bytes 2949120 | tf_op jit(solution)/shard_map/add | solution.py:472
Async XLA Ops:
  0.6 87.9 %copy-start.1 = (f32[64,2560]{1,0:T(8,128)S(1)}, f32[64,2560]{1,0:T(8,128)}, u32[]{:S(2)}) copy-start(f32[64,2560]{1,0:T(8,128)} %param.9) | copy-start | bytes 1966084
  0.6 87.9 %copy-start = (f32[64,2560]{1,0:T(8,128)S(1)}, f32[64,2560]{1,0:T(8,128)}, u32[]{:S(2)}) copy-start(f32[64,2560]{1,0:T(8,128)} %param.8) | copy-start | bytes 1966084

commit v4 on v3

--- a/solution.py
+++ b/solution.py
@@ -201,8 +201,6 @@
     for r in range(1, side):
         remote(kv5.at[:, 0], kv5.at[:, r], kv5f_sent, kv5f_sem, dev(a, minus(b, r, side), z)).start()
 
-    for t in early:
-        sent_q(t)
     lax.fori_loop(1, min(1 + BEFORE, nz), send_kv_layer, 0)
     for t in late:
         send_q(t)
@@ -417,7 +415,7 @@
     for t in range(half):
         await_bytes(o_send.at[t, :, others], o_sent.at[t])
         await_bytes(o_send.at[t, 0, 0], o_sent.at[t])
-    for t in late:
+    for t in tiles:
         sent_q(t)
     delivered(side, 1, out5_sent)
     delivered(0, side, out_sent)

time: 90.8 us -> 90.8 us (level)
  no operation moved by 1% of the time
where the time goes in v4:
time: 90.8 us; the launch traced here: 90.7 us
  Pallas kernels  87.8 us (97%)
  other arithmetic  2.16 us (2%)
    pallas_call x1, Pallas kernels, on_device(): pl.pallas_call(functools.partial(kernel, nz, side, rows), out_shape=jax.S...  87.8 us
    add x1, other arithmetic, on_device(): latent + step_size * (1.5 * velocity - 0.5 * previous_velocity)  2.16 us

profile of v4, /device:TPU:1, one launch (start us, length us, event | category | flops | bytes accessed | tf_op | source)
XLA Modules:
  0.0 90.7 jit_solution(12680308872766987972)
XLA Ops:
  0.6 0.0 copy-start.1
  0.6 0.0 copy-start
  0.7 87.8 %shard_map.68 = bf16[64,2560]{1,0:T(8,128)(2,1)} custom-call(bf16[1,64,5120]{2,1,0:T(8,128)(2,1)} %q_ref.1, bf16[1,64,5120]{2,1,0:T(8,128)(2,1)} %k_ref.1, bf16[1,64,5120]{2,1,0:T(8,128)(2,1)} %v_ref.1), custom_call_target="tpu_custom_call" | custom-call | tf_op jit(solution)/shard_map/pallas_call | solution.py:436
  88.5 0.0 copy-done.1
  88.5 0.0 copy-done
  88.5 2.2 %multiply_add_fusion = (f32[64,2560]{1,0:T(8,128)}, f32[64,2560]{1,0:T(8,128)}) fusion(f32[64,2560]{1,0:T(8,128)S(1)} %copy-done, f32[64,2560]{1,0:T(8,128)S(1)} %copy-done.1, bf16[64,2560]{1,0:T(8,128)(2,1)} %shard_map.68), kind=kLoop, calls=%fused_computation | loop fusion | flops 983040 | bytes 2949120 | tf_op jit(solution)/shard_map/add | solution.py:470
Async XLA Ops:
  0.6 87.9 %copy-start.1 = (f32[64,2560]{1,0:T(8,128)S(1)}, f32[64,2560]{1,0:T(8,128)}, u32[]{:S(2)}) copy-start(f32[64,2560]{1,0:T(8,128)} %param.9) | copy-start | bytes 1966084
  0.6 87.9 %copy-start = (f32[64,2560]{1,0:T(8,128)S(1)}, f32[64,2560]{1,0:T(8,128)}, u32[]{:S(2)}) copy-start(f32[64,2560]{1,0:T(8,128)} %param.8) | copy-start | bytes 1966084
